TPU v7x, 768 devices: a whole 4x8x12 slice. The times are simulated.
768 devices in a mesh: dp: 48 (over x, z), tensor: 16 (over y, core).
Axes of the slice: x: 4, y: 8, z: 12, core: 2. Of those that a mesh axis runs over, the one named last changes fastest.
Arguments:
- query_rows: bfloat16 [12288, 6144], P('dp', 'tensor'), may hold values from -128 to 128
- key_rows: bfloat16 [12288, 6144], P('dp', 'tensor'), may hold values from -5 to 5
- value_rows: bfloat16 [12288, 6144], P('dp', 'tensor'), may hold values from -5 to 5
- out_grad: bfloat16 [12288, 6144], P('dp', 'tensor'), may hold values from -5 to 5
- w_query: bfloat16 [3072, 6144], P(None, 'tensor'), may hold values from -0.375 to 0.375
- w_key: bfloat16 [3072, 6144], P(None, 'tensor'), may hold values from -0.375 to 0.375
- w_value: bfloat16 [3072, 6144], P(None, 'tensor'), may hold values from -0.375 to 0.375
- row_image: int32 [12288], P('dp'), may hold values from 0 to 191, as said below
Outputs:
- input_grad: bfloat16 [12288, 3072], P('dp', 'tensor')
Inputs may be any that keep to these rules, and one draw needn't show every extreme that they name: `row_image`: image numbers fall into groups d * 4 to d * 4 + 3, one for each index d of dp. In each aligned block of 256 rows at most 13 rows carry numbers of any one group; one group has exactly 13 rows in every block.
All inputs are finite; a program needn't handle non-finite values.
Results may differ from a plain program's by a relative error of at most 0.015.
Values may be sent and summed in bfloat16 or wider, within the bound.
A program may use at most 64 MiB of HBM per device.

v0:
```python
import jax
import jax.numpy as jnp
from jax import lax
from jax.sharding import PartitionSpec as P

HEAD = 128
IMG_DEV = 4


def attend_back(queries, keys_in, values_in, grad_out, images):
    row_count = queries.shape[0]
    col_count = queries.shape[1]
    head_count = col_count // HEAD
    scale = HEAD ** (-0.5)
    queries_h = queries.reshape(row_count, head_count, HEAD)
    keys_h = keys_in.reshape(row_count, head_count, HEAD)
    values_h = values_in.reshape(row_count, head_count, HEAD)
    grad_h = grad_out.reshape(row_count, head_count, HEAD)
    scores = (
        jnp.einsum("qhe,khe->hqk", queries_h, keys_h, preferred_element_type=jnp.float32) * scale
    )
    allowed = (images[:, None] == images[None, :])[None, :, :]
    scores = jnp.where(allowed, scores, -1e30)
    highest = jnp.max(scores, axis=2, keepdims=True)
    raised = jnp.where(allowed, jnp.exp(scores - highest), 0.0)
    attention = raised / jnp.sum(raised, axis=2, keepdims=True)
    attention_low = attention.astype(jnp.bfloat16)
    grad_value = jnp.einsum(
        "hqk,qhe->khe", attention_low, grad_h, preferred_element_type=jnp.float32
    ).astype(jnp.bfloat16)
    grad_prob = jnp.einsum("qhe,khe->hqk", grad_h, values_h, preferred_element_type=jnp.float32)
    row_total = jnp.sum(attention * grad_prob, axis=2, keepdims=True)
    dscore = (attention * (grad_prob - row_total) * scale).astype(jnp.bfloat16)
    grad_query = jnp.einsum(
        "hqk,khe->qhe", dscore, keys_h, preferred_element_type=jnp.float32
    ).astype(jnp.bfloat16)
    grad_key = jnp.einsum(
        "hqk,qhe->khe", dscore, queries_h, preferred_element_type=jnp.float32
    ).astype(jnp.bfloat16)
    return (
        grad_query.reshape(row_count, col_count),
        grad_key.reshape(row_count, col_count),
        grad_value.reshape(row_count, col_count),
    )


def shards(query_rows, key_rows, value_rows, out_grad, w_query, w_key, w_value, row_image):
    groups = lax.axis_size("dp")
    row_count = query_rows.shape[0]
    col_count = query_rows.shape[1]
    capacity = 5 * row_count // (2 * groups)
    target = row_image // IMG_DEV
    onehot = (target[:, None] == jnp.arange(groups, dtype=jnp.int32)[None, :]).astype(jnp.int32)
    position = jnp.sum((jnp.cumsum(onehot, axis=0) - 1) * onehot, axis=1)
    placed = target * capacity + position

    def pack_rows(rows_in, empty_value):
        empty = jnp.full((groups * capacity,) + rows_in.shape[1:], empty_value, rows_in.dtype)
        return empty.at[placed].set(rows_in).reshape((groups, capacity) + rows_in.shape[1:])

    arrived = (
        lax.all_to_all(pack_rows(query_rows, 0), "dp", split_axis=0, concat_axis=0, tiled=True),
        lax.all_to_all(pack_rows(key_rows, 0), "dp", split_axis=0, concat_axis=0, tiled=True),
        lax.all_to_all(pack_rows(value_rows, 0), "dp", split_axis=0, concat_axis=0, tiled=True),
        lax.all_to_all(pack_rows(out_grad, 0), "dp", split_axis=0, concat_axis=0, tiled=True),
        lax.all_to_all(pack_rows(row_image, -1), "dp", split_axis=0, concat_axis=0, tiled=True),
    )
    slot_total = groups * capacity
    received = [
        arrived[0].reshape(slot_total, col_count),
        arrived[1].reshape(slot_total, col_count),
        arrived[2].reshape(slot_total, col_count),
        arrived[3].reshape(slot_total, col_count),
        arrived[4].reshape(slot_total),
    ]
    grad_query, grad_key, grad_value = attend_back(
        received[0], received[1], received[2], received[3], received[4]
    )
    contract = (((1,), (1,)), ((), ()))
    returned = (
        lax.all_to_all(
            grad_query.reshape(groups, capacity, col_count),
            "dp",
            split_axis=0,
            concat_axis=0,
            tiled=True,
        ),
        lax.all_to_all(
            grad_key.reshape(groups, capacity, col_count),
            "dp",
            split_axis=0,
            concat_axis=0,
            tiled=True,
        ),
        lax.all_to_all(
            grad_value.reshape(groups, capacity, col_count),
            "dp",
            split_axis=0,
            concat_axis=0,
            tiled=True,
        ),
    )
    own_query = returned[0].reshape(slot_total, col_count)[placed]
    own_key = returned[1].reshape(slot_total, col_count)[placed]
    own_value = returned[2].reshape(slot_total, col_count)[placed]
    summed = lax.dot_general(own_query, w_query, contract, preferred_element_type=jnp.float32)
    summed = summed + lax.dot_general(own_key, w_key, contract, preferred_element_type=jnp.float32)
    partial_value = summed + lax.dot_general(
        own_value, w_value, contract, preferred_element_type=jnp.float32
    )
    summed = lax.psum_scatter(partial_value, "tensor", scatter_dimension=1, tiled=True)
    return summed.astype(jnp.bfloat16)


def solution(mesh):
    placed = (
        P("dp", "tensor"),
        P("dp", "tensor"),
        P("dp", "tensor"),
        P("dp", "tensor"),
        P(None, "tensor"),
        P(None, "tensor"),
        P(None, "tensor"),
        P("dp"),
    )
    return jax.shard_map(
        shards, mesh=mesh, in_specs=placed, out_specs=P("dp", "tensor"), check_vma=False
    )
```

profile of v0, /device:TPU:27, one launch (start us, length us, event | category | flops | bytes accessed | tf_op | source)
XLA Modules:
  0.0 369.5 jit_solution(1472542492791271885)
XLA Ops:
  12.0 17.9 %all-to-all-start.1 = ((s32[48,1,13]{2,1,0:T(1,128)}), s32[48,1,13]{2,1,0:T(1,128)S(1)}, u32[]{:S(2)}, u32[]{:S(2)}) async-start(s32[48,1,13]{2,1,0:T(1,128)} %bitcast.2), calls=%async_computation.1 | async-start | bytes 49152 | tf_op jit(solution)/shard_map/all_to_all | solution.py:66
  29.9 2.0 scatter_custom_fusion.4
  32.9 7.3 %all-to-all-done.1 = s32[48,1,13]{2,1,0:T(1,128)S(1)} async-done(((s32[48,1,13]{2,1,0:T(1,128)}), s32[48,1,13]{2,1,0:T(1,128)S(1)}, u32[]{:S(2)}, u32[]{:S(2)}) %all-to-all-start.1) | async-done | bytes 2528 | tf_op jit(solution)/shard_map/all_to_all | solution.py:66
  40.8 5.3 %all-to-all-start.4 = ((bf16[48,13,384]{2,1,0:T(8,128)(2,1)}), bf16[48,13,384]{2,1,0:T(8,128)(2,1)S(1)}, u32[]{:S(2)}, u32[]{:S(2)}) async-start(bf16[48,13,384]{2,1,0:T(8,128)(2,1)} %reshape.85), calls=%async_computation.4 | async-start | bytes 1179648 | tf_op jit(solution)/shard_map/all_to_all | solution.py:64
  46.1 2.0 scatter_custom_fusion.3
  49.1 20.4 %all-to-all-done.4 = bf16[48,13,384]{2,1,0:T(8,128)(2,1)S(1)} async-done(((bf16[48,13,384]{2,1,0:T(8,128)(2,1)}), bf16[48,13,384]{2,1,0:T(8,128)(2,1)S(1)}, u32[]{:S(2)}, u32[]{:S(2)}) %all-to-all-start.4) | async-done | bytes 479264 | tf_op jit(solution)/shard_map/all_to_all | solution.py:64
  69.5 10.2 %all-to-all-start.3 = ((bf16[48,13,384]{2,1,0:T(8,128)(2,1)}), bf16[48,13,384]{2,1,0:T(8,128)(2,1)S(1)}, u32[]{:S(2)}, u32[]{:S(2)}) async-start(bf16[48,13,384]{2,1,0:T(8,128)(2,1)} %reshape.84), calls=%async_computation.3 | async-start | bytes 1179648 | tf_op jit(solution)/shard_map/all_to_all | solution.py:65
  79.7 2.7 scatter_custom_fusion.2
  82.3 2.0 reshape.83
  84.4 18.6 %all-to-all-done.3 = bf16[48,13,384]{2,1,0:T(8,128)(2,1)S(1)} async-done(((bf16[48,13,384]{2,1,0:T(8,128)(2,1)}), bf16[48,13,384]{2,1,0:T(8,128)(2,1)S(1)}, u32[]{:S(2)}, u32[]{:S(2)}) %all-to-all-start.3) | async-done | bytes 479264 | tf_op jit(solution)/shard_map/all_to_all | solution.py:65
  103.0 10.2 %all-to-all-start.2 = ((bf16[48,13,384]{2,1,0:T(8,128)(2,1)}), bf16[48,13,384]{2,1,0:T(8,128)(2,1)}, u32[]{:S(2)}, u32[]{:S(2)}) async-start(bf16[48,13,384]{2,1,0:T(8,128)(2,1)} %reshape.83), calls=%async_computation.2 | async-start | bytes 1179648 | tf_op jit(solution)/shard_map/all_to_all | solution.py:62
  113.2 2.7 scatter_custom_fusion
  115.8 2.0 reshape.82
  117.9 18.7 %all-to-all-done.2 = bf16[48,13,384]{2,1,0:T(8,128)(2,1)} async-done(((bf16[48,13,384]{2,1,0:T(8,128)(2,1)}), bf16[48,13,384]{2,1,0:T(8,128)(2,1)}, u32[]{:S(2)}, u32[]{:S(2)}) %all-to-all-start.2) | async-done | bytes 479264 | tf_op jit(solution)/shard_map/all_to_all | solution.py:62
  136.6 10.1 %all-to-all-start = ((bf16[48,13,384]{2,1,0:T(8,128)(2,1)}), bf16[48,13,384]{2,1,0:T(8,128)(2,1)}, u32[]{:S(2)}, u32[]{:S(2)}) async-start(bf16[48,13,384]{2,1,0:T(8,128)(2,1)} %reshape.82), calls=%async_computation | async-start | bytes 1179648 | tf_op jit(solution)/shard_map/all_to_all | solution.py:63
  147.2 2.0 reduce.5
  154.9 4.6 %fusion.37 = f32[3,624,624]{1,2,0:T(8,128)} fusion(bf16[624,3,128]{2,1,0:T(4,128)(2,1)} %reshape_reshape.24, bf16[624,3,128]{2,1,0:T(4,128)(2,1)} %reshape_reshape.23), kind=kOutput, calls=%fused_computation.35 | convolution fusion | flops 299040768 | bytes 5630976 | tf_op jit(solution)/shard_map/qhe,khe->hqk/dot_general | solution.py:31
  159.4 10.7 %all-to-all-done = bf16[48,13,384]{2,1,0:T(8,128)(2,1)} async-done(((bf16[48,13,384]{2,1,0:T(8,128)(2,1)}), bf16[48,13,384]{2,1,0:T(8,128)(2,1)}, u32[]{:S(2)}, u32[]{:S(2)}) %all-to-all-start) | async-done | bytes 479264 | tf_op jit(solution)/shard_map/all_to_all | solution.py:63
  170.1 2.2 reshape_reshape.21
  172.3 5.6 %fusion.75 = (f32[3,624]{1,0:T(4,128)S(1)}, f32[3,624,624]{1,2,0:T(8,128)}) fusion(pred[624,624]{0,1:T(8,128)(4,1)S(1)} %copy-done.5, bf16[624,3,128]{2,1,0:T(4,128)(2,1)} %reshape_reshape.21, bf16[624,3,128]{2,1,0:T(4,128)(2,1)S(1)} %reshape_reshape.22), kind=kOutput, calls=%fused_computation.77 | convolution fusion | flops 304882048 | bytes 6027840 | tf_op jit(solution)/shard_map/sub | solution.py:25
  177.9 8.6 %fusion.31 = bf16[624,3,128]{2,0,1:T(8,128)(2,1)S(1)} fusion(f32[3,624,624]{1,2,0:T(8,128)} %fusion.37, bf16[624,3,128]{2,1,0:T(4,128)(2,1)} %reshape_reshape.21, f32[3,624,624]{1,2,0:T(8,128)} %get-tuple-element.6, f32[3,624]{1,0:T(4,128)S(1)} %get-tuple-element.5), kind=kOutput, calls=%fused_computation.32 | convolution fusion | flops 307459776 | bytes 10310976 | tf_op jit(solution)/shard_map/hqk,khe->qhe/dot_general | solution.py:34
  188.0 10.1 %all-to-all-start.5 = ((bf16[48,13,384]{2,1,0:T(8,128)(2,1)}), bf16[48,13,384]{2,1,0:T(8,128)(2,1)}, u32[]{:S(2)}, u32[]{:S(2)}) async-start(bf16[48,13,384]{2,1,0:T(8,128)(2,1)} %reshape_reshape.25), calls=%async_computation.5 | async-start | bytes 1179648 | tf_op jit(solution)/shard_map/all_to_all | solution.py:81
  198.0 8.3 %fusion.28 = bf16[624,3,128]{2,0,1:T(8,128)(2,1)S(1)} fusion(f32[3,624,624]{1,2,0:T(8,128)} %fusion.37, bf16[624,3,128]{2,1,0:T(4,128)(2,1)} %copy-done.4, f32[3,624,624]{1,2,0:T(8,128)} %get-tuple-element.6, f32[3,624]{1,0:T(4,128)S(1)} %get-tuple-element.5), kind=kOutput, calls=%fused_computation.31 | convolution fusion | flops 307459776 | bytes 10310976 | tf_op jit(solution)/shard_map/hqk,qhe->khe/dot_general | solution.py:37
  207.8 13.6 %all-to-all-done.5 = bf16[48,13,384]{2,1,0:T(8,128)(2,1)} async-done(((bf16[48,13,384]{2,1,0:T(8,128)(2,1)}), bf16[48,13,384]{2,1,0:T(8,128)(2,1)}, u32[]{:S(2)}, u32[]{:S(2)}) %all-to-all-start.5) | async-done | bytes 479264 | tf_op jit(solution)/shard_map/all_to_all | solution.py:81
  221.5 10.1 %all-to-all-start.6 = ((bf16[48,13,384]{2,1,0:T(8,128)(2,1)}), bf16[48,13,384]{2,1,0:T(8,128)(2,1)}, u32[]{:S(2)}, u32[]{:S(2)}) async-start(bf16[48,13,384]{2,1,0:T(8,128)(2,1)} %reshape_reshape.26), calls=%async_computation.6 | async-start | bytes 1179648 | tf_op jit(solution)/shard_map/all_to_all | solution.py:88
  231.6 3.4 fusion.34
  236.5 18.5 %all-to-all-done.6 = bf16[48,13,384]{2,1,0:T(8,128)(2,1)} async-done(((bf16[48,13,384]{2,1,0:T(8,128)(2,1)}), bf16[48,13,384]{2,1,0:T(8,128)(2,1)}, u32[]{:S(2)}, u32[]{:S(2)}) %all-to-all-start.6) | async-done | bytes 479264 | tf_op jit(solution)/shard_map/all_to_all | solution.py:88
  255.0 10.0 %all-to-all-start.7 = ((bf16[48,13,384]{2,1,0:T(8,128)(2,1)}), bf16[48,13,384]{2,1,0:T(8,128)(2,1)S(1)}, u32[]{:S(2)}, u32[]{:S(2)}) async-start(bf16[48,13,384]{2,1,0:T(8,128)(2,1)} %reshape_reshape.27), calls=%async_computation.7 | async-start | bytes 1179648 | tf_op jit(solution)/shard_map/all_to_all | solution.py:95
  271.1 17.2 %all-to-all-done.7 = bf16[48,13,384]{2,1,0:T(8,128)(2,1)S(1)} async-done(((bf16[48,13,384]{2,1,0:T(8,128)(2,1)}), bf16[48,13,384]{2,1,0:T(8,128)(2,1)S(1)}, u32[]{:S(2)}, u32[]{:S(2)}) %all-to-all-start.7) | async-done | bytes 479264 | tf_op jit(solution)/shard_map/all_to_all | solution.py:95
  289.7 2.1 fusion.84
  293.5 2.7 convolution_add_fusion
  296.2 64.9 %reduce-scatter.2.cloned.1.call-done = f32[256,192]{0,1:T(8,128)} async-done(((f32[256,3072]{0,1:T(8,128)}), f32[256,192]{0,1:T(8,128)}) %reduce-scatter.2.cloned.1.call-update) | async-done | bytes 196624 | tf_op jit(solution)/shard_map/reduce_scatter | solution.py:111
  (50 shorter events, 29.3 us)
Async XLA Ops:
  6.5 283.2 %copy-start = (bf16[3072,384]{1,0:T(8,128)(2,1)S(1)}, bf16[3072,384]{1,0:T(8,128)(2,1)}, u32[]{:S(2)}) copy-start(bf16[3072,384]{1,0:T(8,128)(2,1)} %param.12) | copy-start | bytes 7077892
  12.0 28.2 %all-to-all-start.1 = ((s32[48,1,13]{2,1,0:T(1,128)}), s32[48,1,13]{2,1,0:T(1,128)S(1)}, u32[]{:S(2)}, u32[]{:S(2)}) async-start(s32[48,1,13]{2,1,0:T(1,128)} %bitcast.2), calls=%async_computation.1 | async-start | bytes 49152 | tf_op jit(solution)/shard_map/all_to_all | solution.py:66
  40.2 0.6 copy-start.6
  40.8 28.7 %all-to-all-start.4 = ((bf16[48,13,384]{2,1,0:T(8,128)(2,1)}), bf16[48,13,384]{2,1,0:T(8,128)(2,1)S(1)}, u32[]{:S(2)}, u32[]{:S(2)}) async-start(bf16[48,13,384]{2,1,0:T(8,128)(2,1)} %reshape.85), calls=%async_computation.4 | async-start | bytes 1179648 | tf_op jit(solution)/shard_map/all_to_all | solution.py:64
  69.5 33.5 %all-to-all-start.3 = ((bf16[48,13,384]{2,1,0:T(8,128)(2,1)}), bf16[48,13,384]{2,1,0:T(8,128)(2,1)S(1)}, u32[]{:S(2)}, u32[]{:S(2)}) async-start(bf16[48,13,384]{2,1,0:T(8,128)(2,1)} %reshape.84), calls=%async_computation.3 | async-start | bytes 1179648 | tf_op jit(solution)/shard_map/all_to_all | solution.py:65
  103.0 33.6 %all-to-all-start.2 = ((bf16[48,13,384]{2,1,0:T(8,128)(2,1)}), bf16[48,13,384]{2,1,0:T(8,128)(2,1)}, u32[]{:S(2)}, u32[]{:S(2)}) async-start(bf16[48,13,384]{2,1,0:T(8,128)(2,1)} %reshape.83), calls=%async_computation.2 | async-start | bytes 1179648 | tf_op jit(solution)/shard_map/all_to_all | solution.py:62
  136.6 33.5 %all-to-all-start = ((bf16[48,13,384]{2,1,0:T(8,128)(2,1)}), bf16[48,13,384]{2,1,0:T(8,128)(2,1)}, u32[]{:S(2)}, u32[]{:S(2)}) async-start(bf16[48,13,384]{2,1,0:T(8,128)(2,1)} %reshape.82), calls=%async_computation | async-start | bytes 1179648 | tf_op jit(solution)/shard_map/all_to_all | solution.py:63
  153.3 19.0 %copy-start.5 = (pred[624,624]{0,1:T(8,128)(4,1)S(1)}, pred[624,624]{0,1:T(8,128)(4,1)}, u32[]{:S(2)}) copy-start(pred[624,624]{0,1:T(8,128)(4,1)} %broadcast_compare_fusion) | copy-start | bytes 1168132
  154.9 23.0 %copy-start.4 = (bf16[624,3,128]{2,1,0:T(4,128)(2,1)}, bf16[624,3,128]{2,1,0:T(4,128)(2,1)S(1)}, u32[]{:S(2)}) copy-start(bf16[624,3,128]{2,1,0:T(4,128)(2,1)S(1)} %reshape_reshape.22) | copy-start | bytes 1437700
  188.0 33.5 %all-to-all-start.5 = ((bf16[48,13,384]{2,1,0:T(8,128)(2,1)}), bf16[48,13,384]{2,1,0:T(8,128)(2,1)}, u32[]{:S(2)}, u32[]{:S(2)}) async-start(bf16[48,13,384]{2,1,0:T(8,128)(2,1)} %reshape_reshape.25), calls=%async_computation.5 | async-start | bytes 1179648 | tf_op jit(solution)/shard_map/all_to_all | solution.py:81
  221.5 33.5 %all-to-all-start.6 = ((bf16[48,13,384]{2,1,0:T(8,128)(2,1)}), bf16[48,13,384]{2,1,0:T(8,128)(2,1)}, u32[]{:S(2)}, u32[]{:S(2)}) async-start(bf16[48,13,384]{2,1,0:T(8,128)(2,1)} %reshape_reshape.26), calls=%async_computation.6 | async-start | bytes 1179648 | tf_op jit(solution)/shard_map/all_to_all | solution.py:88
  255.0 33.4 %all-to-all-start.7 = ((bf16[48,13,384]{2,1,0:T(8,128)(2,1)}), bf16[48,13,384]{2,1,0:T(8,128)(2,1)S(1)}, u32[]{:S(2)}, u32[]{:S(2)}) async-start(bf16[48,13,384]{2,1,0:T(8,128)(2,1)} %reshape_reshape.27), calls=%async_computation.7 | async-start | bytes 1179648 | tf_op jit(solution)/shard_map/all_to_all | solution.py:95
  265.0 96.1 %reduce-scatter.2.cloned.1.call-start = ((), (), s32[]{:S(2)}) async-start(), calls=%async_computation.9 | async-start | bytes 3342336 | tf_op jit(solution)/shard_map/reduce_scatter | solution.py:111
  288.5 3.3 copy-start.3
  289.7 2.1 copy-start.1
  291.8 1.7 copy-start.2
Sparse Core Ops, SparseCore 0:
  296.3 64.7 reduce-scatter.1
where the time goes:
time: 371 us; the launch traced here: 370 us
  waiting for transfers between devices  190 us (51%)
  starting transfers between devices  83.8 us (23%)
  local copies, waits for them, and re-layouts  38.3 us (10%)
  matrix products  36.2 us (10%)
  between operations  13.6 us (4%)
  other arithmetic  7.63 us (2%)
    reduce_scatter x1, waiting for transfers between devices, shards(): lax.psum_scatter(partial_value, 'tensor', scatter_dimension=1, tiled=True)  64.9 us
    all_to_all x1, waiting for transfers between devices, shards(): lax.all_to_all(pack_rows(value_rows, 0), 'dp', split_axis=0, concat_axis=...  20.4 us
    all_to_all x1, waiting for transfers between devices, shards(): lax.all_to_all(pack_rows(query_rows, 0), 'dp', split_axis=0, concat_axis=...  18.7 us
    all_to_all x1, waiting for transfers between devices, shards(): lax.all_to_all(pack_rows(out_grad, 0), 'dp', split_axis=0, concat_axis=0,...  18.6 us
    all_to_all x1, waiting for transfers between devices, shards(): lax.all_to_all(grad_key.reshape(groups, capacity, col_count), 'dp', split...  18.5 us
    all_to_all x1, starting transfers between devices, shards(): lax.all_to_all(pack_rows(row_image, -1), 'dp', split_axis=0, concat_axis=...  17.9 us
    all_to_all x1, waiting for transfers between devices, shards(): lax.all_to_all(grad_value.reshape(groups, capacity, col_count), 'dp', spl...  17.2 us
    all_to_all x1, waiting for transfers between devices, shards(): lax.all_to_all(grad_query.reshape(groups, capacity, col_count), 'dp', spl...  13.6 us
  transfers between devices with their start and end apart: 9, of which 9 were waited for; matrix products, arithmetic and copies ran while one was open for 13% of the time, Pallas kernels for 0%

commit v1 on v0

v1 whole, which is shorter than its diff:
```python
import functools

import jax
import jax.numpy as jnp
from jax import lax
from jax.experimental import pallas as pl
from jax.experimental.pallas import tpu as pltpu
from jax.sharding import PartitionSpec as P

HEAD = 128
IMG_DEV = 4
CAP = 13
PAD = 16
TOGETHER = 6
WINDOW = 32
BLOCK_ROWS = 160
CODE_ROW = 156
GROUP_ROWS = 80
MESH = pl.DeviceIdType.MESH
F32 = jnp.float32
BF16 = jnp.bfloat16


def iota(shape, dim):
    return lax.broadcasted_iota(jnp.int32, shape, dim)


def dot(a, b, contract=((1,), (0,))):
    return lax.dot_general(a, b, (contract, ((), ())), preferred_element_type=F32)


def kernel(
    sizes,
    image_row,
    image_col,
    query,
    key,
    value,
    grad,
    w_query,
    w_key,
    w_value,
    out,
    codes,
    position,
    send,
    recv,
    blocks,
    mask_row,
    mask_col,
    grads,
    weights,
    own,
    sib_send,
    sib_recv,
    ring_send,
    ring_recv,
    back_send,
    back_recv,
    last_send,
    last_recv,
    send_sem,
    recv_sem,
    weight_sem,
    sib_send_sem,
    sib_recv_sem,
    ring_send_sem,
    ring_recv_sem,
    back_send_sem,
    back_recv_sem,
    last_sem,
):
    n_dp, n_y = sizes
    tokens = query.shape[0]
    cols = query.shape[1]
    heads = cols // HEAD
    n_blocks = 4 * heads
    n_groups = n_dp // TOGETHER
    slots = n_groups * GROUP_ROWS
    chains = n_groups // 2
    upward = chains // 2
    chip_cols = out.shape[1] * 2
    me = lax.axis_index("dp")
    lane = lax.axis_index("tensor")
    core = lane % 2
    y = lane // 2
    sibling = y * 2 + (1 - core)
    above = lax.rem(y + 1, n_y) * 2 + core
    below = lax.rem(y + n_y - 1, n_y) * 2 + core

    barrier = pltpu.get_barrier_semaphore()

    def greet(step, carry):
        pl.semaphore_signal(
            barrier,
            inc=1,
            device_id=(lax.rem(me + step, n_dp), lane),
            device_id_type=MESH,
        )
        return carry

    lax.fori_loop(1, n_dp, greet, 0)
    for other in (sibling, above, below):
        pl.semaphore_signal(barrier, inc=1, device_id=(me, other), device_id_type=MESH)

    weight_copies = [
        pltpu.make_async_copy(source, weights.at[:, pl.ds(i * cols, cols)], weight_sem.at[i])
        for i, source in enumerate((w_query, w_key, w_value))
    ]
    for copy in weight_copies:
        copy.start()

    img_r = image_row[...]
    target_r = img_r >> 2
    hit_r = jnp.where(iota((n_dp, tokens), 0) == target_r, 1.0, 0.0)
    upper = jnp.where(
        iota((tokens, tokens), 0) < iota((tokens, tokens), 1), 1.0, 0.0
    ).astype(BF16)
    before_r = dot(hit_r.astype(BF16), upper)
    pos_r = jnp.sum(before_r * hit_r, axis=0, keepdims=True)
    placed_r = target_r.astype(F32) * PAD + pos_r
    img_c = image_col[...]
    target_c = img_c >> 2
    hit_c = jnp.where(iota((tokens, n_dp), 1) == target_c, 1.0, 0.0)
    lower = jnp.where(
        iota((tokens, tokens), 1) < iota((tokens, tokens), 0), 1.0, 0.0
    ).astype(BF16)
    before_c = dot(lower, hit_c.astype(BF16))
    pos_c = jnp.sum(before_c * hit_c, axis=1, keepdims=True)
    position[...] = target_c.astype(F32) * PAD + pos_c

    code_r = ((img_r & 3) + 1).astype(F32)
    shift = (lax.rem(me, TOGETHER) * CAP).astype(F32)
    place = jnp.where(
        iota((tokens, HEAD), 1).astype(F32) == pos_c + shift, 1.0, 0.0
    ).astype(BF16)
    codes[...] = dot((hit_r * code_r).astype(BF16), place)

    tight_out = iota((BLOCK_ROWS, n_blocks * PAD), 0)
    tight_in = iota((BLOCK_ROWS, n_blocks * PAD), 1)
    tight = jnp.where(
        (tight_out == (tight_in >> 4) * CAP + (tight_in & 15)) & ((tight_in & 15) < CAP),
        1.0,
        0.0,
    ).astype(BF16)

    def pack(step, carry):
        some = TOGETHER * PAD
        wanted = (iota((some, tokens), 0) + step * some).astype(F32)
        pick = jnp.where(wanted == placed_r, 1.0, 0.0).astype(BF16)
        parts = [dot(pick, ref[...]).astype(BF16) for ref in (query, key, value, grad)]
        rows = []
        for block in range(n_blocks):
            part = parts[block // heads]
            left = (block % heads) * HEAD
            rows.append(
                jnp.concatenate(
                    [
                        part[i * PAD : (i + 1) * PAD, left : left + HEAD]
                        for i in range(TOGETHER)
                    ],
                    axis=1,
                )
            )
        packed = dot(tight, jnp.concatenate(rows, axis=0))
        code = jnp.concatenate(
            [codes[pl.ds(step * TOGETHER + i, 1), :] for i in range(TOGETHER)], axis=1
        )
        packed = jnp.where(iota(packed.shape, 0) == CODE_ROW, code, packed).astype(BF16)
        for i in range(TOGETHER):
            send[step * TOGETHER + i] = packed[:, i * HEAD : (i + 1) * HEAD]
        return carry

    lax.fori_loop(0, n_groups, pack, 0)

    pl.semaphore_wait(barrier, n_dp + 2)

    def message(place_in, target):
        return pltpu.make_async_remote_copy(
            src_ref=send.at[target],
            dst_ref=recv.at[place_in],
            send_sem=send_sem.at[target],
            recv_sem=recv_sem.at[place_in],
            device_id=(target, lane),
            device_id_type=MESH,
        )

    def start_message(step, carry):
        message(me, lax.rem(me + step, n_dp)).start()
        return carry

    lax.fori_loop(1, n_dp, start_message, 0)
    recv[me] = send[me]
    for copy in weight_copies:
        copy.wait()

    def wait_message(step, carry):
        other = lax.rem(me + step, n_dp)
        message(other, other).wait_recv()
        return carry

    lax.fori_loop(1, n_dp, wait_message, 0)

    for block in range(n_blocks):
        top = block * CAP // 16 * 16
        skip = block * CAP - top
        shape = (GROUP_ROWS, TOGETHER * WINDOW)
        to, source = iota(shape, 0), iota(shape, 1)
        within = (source & (WINDOW - 1)) - skip
        loose = jnp.where(
            (to == (source >> 5) * CAP + within) & (within >= 0) & (within < CAP), 1.0, 0.0
        ).astype(BF16)
        wide = jnp.concatenate(
            [
                jnp.concatenate(
                    [recv[g * TOGETHER + i, top : top + WINDOW, :] for g in range(n_groups)],
                    axis=1,
                )
                for i in range(TOGETHER)
            ],
            axis=0,
        )
        spread = dot(loose, wide).astype(BF16)
        for g in range(n_groups):
            blocks[block, g * GROUP_ROWS : (g + 1) * GROUP_ROWS, :] = spread[
                :, g * HEAD : (g + 1) * HEAD
            ]

    total = None
    for g in range(n_groups):
        tile = recv[g * TOGETHER, CODE_ROW - 12 :, :].astype(F32)
        for i in range(1, TOGETHER):
            tile = tile + recv[g * TOGETHER + i, CODE_ROW - 12 :, :].astype(F32)
        only = jnp.where(iota((16, HEAD), 0) == 12, tile, 0.0).astype(BF16)
        shape = (HEAD, slots)
        there = iota(shape, 0)
        put = jnp.where(
            (iota(shape, 1) == g * GROUP_ROWS + there) & (there < GROUP_ROWS), 1.0, 0.0
        ).astype(BF16)
        term = dot(only, put)
        total = term if total is None else total + term
    code_row = jnp.sum(total, axis=0, keepdims=True)
    mask_row[...] = code_row
    mask_col[...] = jnp.transpose(jnp.broadcast_to(code_row, (HEAD, slots)))

    scale = HEAD ** (-0.5)
    last = ((1,), (1,))

    def attend(head, carry):
        q = blocks[head]
        k = blocks[heads + head]
        v = blocks[2 * heads + head]
        g = blocks[3 * heads + head]
        allowed = mask_col[:, 0:1] == mask_row[...]
        scores = jnp.where(allowed, dot(k, q, last), -1e30)
        highest = jnp.max(scores, axis=0, keepdims=True)
        raised = jnp.exp((scores - highest) * scale)
        attention = raised * (1.0 / jnp.sum(raised, axis=0, keepdims=True))
        grad_prob = dot(v, g, last)
        row_total = jnp.sum(attention * grad_prob, axis=0, keepdims=True)
        dscore = (attention * (grad_prob - row_total) * scale).astype(BF16)
        grad_value = dot(attention.astype(BF16), g).astype(BF16)
        grad_key = dot(dscore, q).astype(BF16)
        grad_query = jnp.transpose(dot(k, dscore, ((0,), (0,)))).astype(BF16)
        half = slots // 2
        for i, result in enumerate((grad_query, grad_key, grad_value)):
            left = pl.multiple_of((i * heads + head) * HEAD, HEAD)
            grads[0, :, pl.ds(left, HEAD)] = result[:half]
            grads[1, :, pl.ds(left, HEAD)] = result[half:]
        return carry

    lax.fori_loop(0, heads, attend, 0)

    def to_sibling(step):
        return pltpu.make_async_remote_copy(
            src_ref=sib_send.at[step],
            dst_ref=sib_recv.at[step],
            send_sem=sib_send_sem.at[step],
            recv_sem=sib_recv_sem.at[step],
            device_id=(me, sibling),
            device_id_type=MESH,
        )

    def project(step):
        for way in range(2):
            if way == 0:
                chunk = lax.rem(y + 2 * n_y - 1 - step, n_y)
            else:
                chunk = lax.rem(y + 1 + step, n_y)
            w = weights[pl.ds(pl.multiple_of(chunk * chip_cols, chip_cols), chip_cols), :]
            half = upward * GROUP_ROWS
            top = way * half
            rows = jnp.concatenate(
                [grads[core, top : top + half, :], grads[1 - core, top : top + half, :]],
                axis=0,
            )
            product = dot(rows, w, last)
            for i in range(upward):
                chain = way * upward + i
                here = product[i * GROUP_ROWS : (i + 1) * GROUP_ROWS]
                there = product[half + i * GROUP_ROWS : half + (i + 1) * GROUP_ROWS]
                own[step, chain] = here
                sib_send[step, chain] = there.astype(BF16)
        to_sibling(step).start()

    def hop(step, chain):
        slot = step * chains + chain
        return pltpu.make_async_remote_copy(
            src_ref=ring_send.at[slot],
            dst_ref=ring_recv.at[slot],
            send_sem=ring_send_sem.at[slot],
            recv_sem=ring_recv_sem.at[slot],
            device_id=(me, above if chain < upward else below),
            device_id_type=MESH,
        )

    def running(step, chain):
        return own[step, chain] + sib_recv[step, chain].astype(F32)

    project(0)
    project(1)
    to_sibling(0).wait_recv()
    for chain in range(chains):
        ring_send[chain] = running(0, chain).astype(BF16)
        hop(0, chain).start()

    def ring_step(step, carry):
        @pl.when(step < n_y - 1)
        def _():
            project(step + 1)

        to_sibling(step).wait_recv()
        for pair in range(upward):
            for chain in (pair, upward + pair):
                hop(step - 1, chain).wait_recv()
                before = (step - 1) * chains + chain
                ring_send[step * chains + chain] = (
                    running(step, chain) + ring_recv[before].astype(F32)
                ).astype(BF16)
                hop(step, chain).start()
        return carry

    lax.fori_loop(1, n_y - 1, ring_step, 0)

    def back(index, target, home):
        return pltpu.make_async_remote_copy(
            src_ref=back_send.at[index],
            dst_ref=back_recv.at[home],
            send_sem=back_send_sem.at[index],
            recv_sem=back_recv_sem.at[home],
            device_id=(target, lane),
            device_id_type=MESH,
        )

    shape = (TOGETHER * PAD, GROUP_ROWS)
    to, source = iota(shape, 0), iota(shape, 1)
    apart = jnp.where(
        (source == (to >> 4) * CAP + (to & 15)) & ((to & 15) < CAP), 1.0, 0.0
    ).astype(BF16)
    to_sibling(n_y - 1).wait_recv()
    for pair in range(upward):
        for chain in (pair, upward + pair):
            hop(n_y - 2, chain).wait_recv()
            before = (n_y - 2) * chains + chain
            final = (running(n_y - 1, chain) + ring_recv[before].astype(F32)).astype(BF16)
            laid = dot(apart, final).astype(BF16)
            for i in range(TOGETHER):
                index = chain * TOGETHER + i
                target = (core * chains + chain) * TOGETHER + i
                back_send[index] = laid[i * PAD : (i + 1) * PAD]

                @pl.when(target != me)
                def _():
                    back(index, target, me).start()

                @pl.when(target == me)
                def _():
                    back_recv[me] = back_send[index]

    half_dp = n_dp // 2
    mine = (me // half_dp) == core

    def to_last():
        return pltpu.make_async_remote_copy(
            src_ref=last_send,
            dst_ref=last_recv,
            send_sem=last_sem.at[0],
            recv_sem=last_sem.at[1],
            device_id=(me, sibling),
            device_id_type=MESH,
        )

    @pl.when(mine)
    def _():
        def wait_back(step, carry):
            home = lax.rem(me + step, n_dp)
            back(0, home, home).wait_recv()
            return carry

        lax.fori_loop(1, n_dp, wait_back, 0)
        width = out.shape[1]
        wide = last_send.shape[1]
        pick = jnp.where(
            iota((tokens, n_dp * PAD), 1).astype(F32) == position[...], 1.0, 0.0
        ).astype(BF16)
        every = back_recv[...].reshape(n_dp * PAD, chip_cols)
        rows = dot(pick, every).astype(BF16)
        shape = (chip_cols, wide)
        from_col, to_col = iota(shape, 0), iota(shape, 1)
        other = jnp.where(
            (from_col == to_col + (1 - core) * width) & (to_col < width), 1.0, 0.0
        ).astype(BF16)
        here = jnp.where(
            (from_col == to_col + core * width) & (to_col < width), 1.0, 0.0
        ).astype(BF16)
        last_send[...] = dot(rows, other).astype(BF16)
        to_last().start()
        out[...] = dot(rows, here)[:, :width].astype(BF16)
        to_last().wait_send()

    @pl.when(jnp.logical_not(mine))
    def _():
        to_last().wait_recv()
        out[...] = last_recv[:, : out.shape[1]]

    def left_message(step, carry):
        other = lax.rem(me + step, n_dp)
        message(other, other).wait_send()
        return carry

    lax.fori_loop(1, n_dp, left_message, 0)

    def left_step(step, carry):
        to_sibling(step).wait_send()
        return carry

    lax.fori_loop(0, n_y, left_step, 0)

    def left_hop(step, carry):
        for chain in range(chains):
            hop(step, chain).wait_send()
        return carry

    lax.fori_loop(0, n_y - 1, left_hop, 0)

    def left_back(index, carry):
        target = core * half_dp + index

        @pl.when(target != me)
        def _():
            back(index, target, me).wait_send()

        return carry

    lax.fori_loop(0, half_dp, left_back, 0)


def shards(query_rows, key_rows, value_rows, out_grad, w_query, w_key, w_value, row_image):
    n_dp = lax.axis_size("dp")
    n_tensor = lax.axis_size("tensor")
    n_y = n_tensor // 2
    tokens, cols = query_rows.shape
    features = w_query.shape[0]
    width = features // n_tensor
    chip_cols = 2 * width
    wide = (width + HEAD - 1) // HEAD * HEAD
    heads = cols // HEAD
    n_groups = n_dp // TOGETHER
    slots = n_groups * GROUP_ROWS
    chains = n_groups // 2
    vmem = pl.BlockSpec(memory_space=pltpu.VMEM)
    hbm = pl.BlockSpec(memory_space=pl.ANY)
    dma = pltpu.SemaphoreType.DMA
    return pl.pallas_call(
        functools.partial(kernel, (n_dp, n_y)),
        out_shape=jax.ShapeDtypeStruct((tokens, width), BF16),
        in_specs=[vmem] * 6 + [hbm] * 3,
        out_specs=vmem,
        scratch_shapes=[
            pltpu.VMEM((n_dp, HEAD), F32),
            pltpu.VMEM((tokens, 1), F32),
            pltpu.VMEM((n_dp, BLOCK_ROWS, HEAD), BF16),
            pltpu.VMEM((n_dp, BLOCK_ROWS, HEAD), BF16),
            pltpu.VMEM((4 * heads, slots, HEAD), BF16),
            pltpu.VMEM((1, slots), F32),
            pltpu.VMEM((slots, HEAD), F32),
            pltpu.VMEM((2, slots // 2, 3 * cols), BF16),
            pltpu.VMEM((features, 3 * cols), BF16),
            pltpu.VMEM((n_y, chains, GROUP_ROWS, chip_cols), F32),
            pltpu.VMEM((n_y, chains, GROUP_ROWS, chip_cols), BF16),
            pltpu.VMEM((n_y, chains, GROUP_ROWS, chip_cols), BF16),
            pltpu.VMEM(((n_y - 1) * chains, GROUP_ROWS, chip_cols), BF16),
            pltpu.VMEM(((n_y - 1) * chains, GROUP_ROWS, chip_cols), BF16),
            pltpu.VMEM((n_dp // 2, PAD, chip_cols), BF16),
            pltpu.VMEM((n_dp, PAD, chip_cols), BF16),
            pltpu.VMEM((tokens, wide), BF16),
            pltpu.VMEM((tokens, wide), BF16),
            dma((n_dp,)),
            dma((n_dp,)),
            dma((3,)),
            dma((n_y,)),
            dma((n_y,)),
            dma(((n_y - 1) * chains,)),
            dma(((n_y - 1) * chains,)),
            dma((n_dp // 2,)),
            dma((n_dp,)),
            dma((2,)),
        ],
        compiler_params=pltpu.CompilerParams(
            collective_id=0, has_side_effects=True, vmem_limit_bytes=56 * 2**20
        ),
    )(
        row_image.reshape(1, tokens),
        row_image.reshape(tokens, 1),
        query_rows,
        key_rows,
        value_rows,
        out_grad,
        w_query,
        w_key,
        w_value,
    )


def solution(mesh):
    placed = (
        P("dp", "tensor"),
        P("dp", "tensor"),
        P("dp", "tensor"),
        P("dp", "tensor"),
        P(None, "tensor"),
        P(None, "tensor"),
        P(None, "tensor"),
        P("dp"),
    )
    return jax.shard_map(
        shards, mesh=mesh, in_specs=placed, out_specs=P("dp", "tensor"), check_vma=False
    )
```

time: 371 us -> 144 us (0.39)
  the two profiles are of different devices: /device:TPU:27 before, /device:TPU:3 now
where the time goes in v1:
time: 144 us
  Pallas kernels  141 us (98%)
  local copies, waits for them, and re-layouts  3.1 us (2%)
    pallas_call x1, Pallas kernels, shards(): pl.pallas_call(functools.partial(kernel, (n_dp, n_y)), out_shape=jax.Shap...  141 us

profile of v1, /device:TPU:3, one launch (start us, length us, event | category | flops | bytes accessed | tf_op | source)
XLA Modules:
  0.0 143.7 jit_solution(10565411612620229108)
XLA Ops:
  0.0 1.5 %copy.10.image_col = s32[256,1]{1,0:T(8,128)} copy(s32[256,1]{0,1:T(1,128)} %bitcast.2) | data formatting | bytes 2048 | tf_op jit(solution)/shard_map/reshape | solution.py:514
  1.5 140.6 %shard_map.82 = bf16[256,192]{1,0:T(8,128)(2,1)} custom-call(s32[1,256]{1,0:T(1,128)} %bitcast.3, s32[256,1]{1,0:T(8,128)} %copy.10.image_col, bf16[256,384]{1,0:T(8,128)(2,1)} %query.1, bf16[256,384]{1,0:T(8,128)(2,1)} %key.1, bf16[256,384]{1,0:T(8,128)(2,1)} %value.1, bf16[256,384]{1,0:T(8,128)(2,1)} %grad.1, bf16[3072,384]{1,0:T(8,128)(2,1)} %w_query.1, ...), custom_call_target="tpu_custom_call" | custom-call | tf_op jit(solution)/shard_map/pallas_call | solution.py:474
  142.1 1.6 %copy.11 = bf16[256,192]{0,1:T(8,128)(2,1)} copy(bf16[256,192]{1,0:T(8,128)(2,1)} %shard_map.82) | data formatting | bytes 196608 | tf_op jit(solution)/shard_map/pallas_call | solution.py:474

commit v2 on v1

v2 whole, which is shorter than its diff:
```python
import functools

import jax
import jax.numpy as jnp
from jax import lax
from jax.experimental import pallas as pl
from jax.experimental.pallas import tpu as pltpu
from jax.sharding import PartitionSpec as P

HEAD = 128
IMG_DEV = 4
CAP = 13
PAD = 16
TOGETHER = 6
WINDOW = 32
BLOCK_ROWS = 160
PARTS = ((0, 64), (64, 48), (112, 48))
GROUP_ROWS = 80
MESH = pl.DeviceIdType.MESH
F32 = jnp.float32
BF16 = jnp.bfloat16


def iota(shape, dim):
    return lax.broadcasted_iota(jnp.int32, shape, dim)


def dot(a, b, contract=((1,), (0,))):
    return lax.dot_general(a, b, (contract, ((), ())), preferred_element_type=F32)


def kernel(
    sizes,
    image_row,
    query,
    key,
    value,
    grad,
    w_query,
    w_key,
    w_value,
    out,
    codes,
    position,
    send,
    recv,
    blocks,
    mask_row,
    mask_col,
    grad_mine,
    grad_send,
    grad_recv,
    weights,
    sums,
    ring_send,
    ring_recv,
    back_send,
    back_recv,
    last_send,
    last_recv,
    send_sem,
    recv_sem,
    weight_sem,
    far_send_sem,
    far_recv_sem,
    grad_send_sem,
    grad_recv_sem,
    ring_send_sem,
    ring_recv_sem,
    back_send_sem,
    back_recv_sem,
    last_sem,
):
    n_dp, n_y = sizes
    tokens = query.shape[0]
    cols = query.shape[1]
    heads = cols // HEAD
    n_blocks = 4 * heads
    n_groups = n_dp // TOGETHER
    slots = n_groups * GROUP_ROWS
    half_slots = slots // 2
    chains = n_groups // 2
    upward = chains // 2
    chip_cols = out.shape[1] * 2
    me = lax.axis_index("dp")
    lane = lax.axis_index("tensor")
    core = lane % 2
    y = lane // 2
    sibling = y * 2 + (1 - core)
    above = lax.rem(y + 1, n_y) * 2 + core
    below = lax.rem(y + n_y - 1, n_y) * 2 + core

    barrier = pltpu.get_barrier_semaphore()

    def greet(step, carry):
        pl.semaphore_signal(
            barrier,
            inc=1,
            device_id=(lax.rem(me + step, n_dp), lane),
            device_id_type=MESH,
        )
        return carry

    lax.fori_loop(1, n_dp, greet, 0)
    for other in (sibling, above, below):
        pl.semaphore_signal(barrier, inc=1, device_id=(me, other), device_id_type=MESH)

    sources = (w_query, w_key, w_value)
    weight_copies = [
        pltpu.make_async_copy(
            source, weights.at[0, :, pl.ds(i * cols, cols)], weight_sem.at[i]
        )
        for i, source in enumerate(sources)
    ]
    far_copies = [
        pltpu.make_async_remote_copy(
            src_ref=source,
            dst_ref=weights.at[1, :, pl.ds(i * cols, cols)],
            send_sem=far_send_sem.at[i],
            recv_sem=far_recv_sem.at[i],
            device_id=(me, sibling),
            device_id_type=MESH,
        )
        for i, source in enumerate(sources)
    ]

    img_r = image_row[...]
    target_r = img_r >> 2
    hit_r = jnp.where(iota((n_dp, tokens), 0) == target_r, 1.0, 0.0)
    upper = jnp.where(
        iota((tokens, tokens), 0) < iota((tokens, tokens), 1), 1.0, 0.0
    ).astype(BF16)
    before_r = dot(hit_r.astype(BF16), upper)
    pos_r = jnp.sum(before_r * hit_r, axis=0, keepdims=True)
    placed_r = target_r.astype(F32) * PAD + pos_r
    code_r = ((img_r & 3) + 1).astype(F32)
    shift = (lax.rem(me, TOGETHER) * CAP).astype(F32)
    place = jnp.where(
        iota((HEAD, tokens), 0).astype(F32) == pos_r + shift, 1.0, 0.0
    ).astype(BF16)
    last = ((1,), (1,))
    codes[...] = dot((hit_r * code_r).astype(BF16), place, last)

    tight_out = iota((BLOCK_ROWS, n_blocks * PAD), 0)
    tight_in = iota((BLOCK_ROWS, n_blocks * PAD), 1)
    tight = jnp.where(
        (tight_out == 1 + (tight_in >> 4) * CAP + (tight_in & 15)) & ((tight_in & 15) < CAP),
        1.0,
        0.0,
    ).astype(BF16)

    def message(part, place_in, target):
        rows = pl.ds(*PARTS[part])
        return pltpu.make_async_remote_copy(
            src_ref=send.at[target, rows],
            dst_ref=recv.at[place_in, rows],
            send_sem=send_sem.at[part, target],
            recv_sem=recv_sem.at[part, place_in],
            device_id=(target, lane),
            device_id_type=MESH,
        )

    pl.semaphore_wait(barrier, n_dp + 2)

    def pack(step, carry):
        targets = [lax.rem(me + 1 + step * TOGETHER + i, n_dp) for i in range(TOGETHER)]
        wanted = jnp.concatenate(
            [iota((PAD, tokens), 0) + target * PAD for target in targets], axis=0
        ).astype(F32)
        pick = jnp.where(wanted == placed_r, 1.0, 0.0).astype(BF16)
        parts = [dot(pick, ref[...]).astype(BF16) for ref in (query, key, value, grad)]
        rows = []
        for head in range(heads):
            for part in parts:
                rows.append(
                    jnp.concatenate(
                        [
                            part[i * PAD : (i + 1) * PAD, head * HEAD : (head + 1) * HEAD]
                            for i in range(TOGETHER)
                        ],
                        axis=1,
                    )
                )
        packed = dot(tight, jnp.concatenate(rows, axis=0))
        code = jnp.concatenate([codes[pl.ds(target, 1), :] for target in targets], axis=1)
        packed = jnp.where(iota(packed.shape, 0) == 0, code, packed).astype(BF16)
        for i, target in enumerate(targets):
            send[target] = packed[:, i * HEAD : (i + 1) * HEAD]

            @pl.when(target != me)
            def _():
                message(0, me, target).start()

        return carry

    lax.fori_loop(0, n_groups, pack, 0)
    for copy in weight_copies + far_copies:
        copy.start()
    for part in range(1, heads):

        def start_part(step, carry):
            message(part, me, lax.rem(me + step, n_dp)).start()
            return carry

        lax.fori_loop(1, n_dp, start_part, 0)
    recv[me] = send[me]
    position[...] = jnp.transpose(jnp.broadcast_to(placed_r, (HEAD, tokens)))

    def unpack(head):
        def one(which, carry):
            start = 1 + (head * 4 + which) * CAP
            top = pl.multiple_of(jnp.minimum(start // 16 * 16, BLOCK_ROWS - WINDOW), 16)
            skip = start - top
            shape = (GROUP_ROWS, TOGETHER * WINDOW)
            to, source = iota(shape, 0), iota(shape, 1)
            within = (source & (WINDOW - 1)) - skip
            loose = jnp.where(
                (to == (source >> 5) * CAP + within) & (within >= 0) & (within < CAP),
                1.0,
                0.0,
            ).astype(BF16)
            wide = jnp.concatenate(
                [
                    jnp.concatenate(
                        [
                            recv[g * TOGETHER + i, pl.ds(top, WINDOW), :]
                            for g in range(n_groups)
                        ],
                        axis=1,
                    )
                    for i in range(TOGETHER)
                ],
                axis=0,
            )
            spread = dot(loose, wide).astype(BF16)
            for g in range(n_groups):
                blocks[which, g * GROUP_ROWS : (g + 1) * GROUP_ROWS, :] = spread[
                    :, g * HEAD : (g + 1) * HEAD
                ]
            return carry

        lax.fori_loop(0, 4, one, 0)

    def codes_in():
        total = None
        for g in range(n_groups):
            tile = recv[g * TOGETHER, :16, :].astype(F32)
            for i in range(1, TOGETHER):
                tile = tile + recv[g * TOGETHER + i, :16, :].astype(F32)
            only = jnp.where(iota((16, HEAD), 0) == 0, tile, 0.0).astype(BF16)
            shape = (HEAD, slots)
            there = iota(shape, 0)
            put = jnp.where(
                (iota(shape, 1) == g * GROUP_ROWS + there) & (there < GROUP_ROWS), 1.0, 0.0
            ).astype(BF16)
            term = dot(only, put)
            total = term if total is None else total + term
        code_row = jnp.sum(total, axis=0, keepdims=True)
        mask_row[...] = code_row
        mask_col[...] = jnp.transpose(jnp.broadcast_to(code_row, (HEAD, slots)))

    scale = HEAD ** (-0.5)

    def to_sibling(head):
        return pltpu.make_async_remote_copy(
            src_ref=grad_send.at[head],
            dst_ref=grad_recv.at[head],
            send_sem=grad_send_sem.at[head],
            recv_sem=grad_recv_sem.at[head],
            device_id=(me, sibling),
            device_id_type=MESH,
        )

    def attend(head):
        q = blocks[0]
        k = blocks[1]
        v = blocks[2]
        g = blocks[3]
        allowed = mask_col[:, 0:1] == mask_row[...]
        scores = jnp.where(allowed, dot(k, q, last), -1e30)
        highest = jnp.max(scores, axis=0, keepdims=True)
        raised = jnp.exp((scores - highest) * scale)
        attention = raised * (1.0 / jnp.sum(raised, axis=0, keepdims=True))
        grad_prob = dot(v, g, last)
        row_total = jnp.sum(attention * grad_prob, axis=0, keepdims=True)
        dscore = (attention * (grad_prob - row_total) * scale).astype(BF16)
        grad_value = dot(attention.astype(BF16), g).astype(BF16)
        grad_key = dot(dscore, q).astype(BF16)
        grad_query = jnp.transpose(dot(k, dscore, ((0,), (0,)))).astype(BF16)
        first = core == 0
        for i, result in enumerate((grad_query, grad_key, grad_value)):
            low, high = result[:half_slots], result[half_slots:]
            left = slice(i * HEAD, (i + 1) * HEAD)
            grad_mine[head, :, left] = jnp.where(first, low, high)
            grad_send[head, :, left] = jnp.where(first, high, low)
        to_sibling(head).start()

    def chunk_of(o):
        ahead = (n_y - o) // 2
        return lax.rem(y + n_y + jnp.where(o % 2 == 1, -ahead, ahead), n_y)

    def product(source, owner, o, some):
        left = pl.multiple_of(chunk_of(o) * chip_cols, chip_cols)
        rows = jnp.concatenate([source[head] for head in some], axis=1)
        w = jnp.concatenate(
            [
                weights[
                    owner,
                    pl.ds(left, chip_cols),
                    i * cols + head * HEAD : i * cols + (head + 1) * HEAD,
                ]
                for head in some
                for i in range(3)
            ],
            axis=1,
        )
        return dot(rows, w, last)

    def project_first(o, carry):
        early = range(heads - 1)
        sums[o] = product(grad_mine, 0, o, early) + product(grad_recv, 1, o, early)
        return carry

    def project_last(o, carry):
        some = (heads - 1,)
        sums[o] += product(grad_mine, 0, o, some) + product(grad_recv, 1, o, some)
        return carry

    def one_head(head, carry):
        for part in range(heads):

            @pl.when(head == part)
            def _():
                def wait_part(step, carry):
                    other = lax.rem(me + step, n_dp)
                    message(part, other, other).wait_recv()
                    return carry

                lax.fori_loop(1, n_dp, wait_part, 0)

        unpack(head)
        pl.when(head == 0)(codes_in)
        attend(head)

        @pl.when(head == heads - 2)
        def _():
            for copy in weight_copies:
                copy.wait()
            for copy in far_copies:
                copy.wait_recv()
            for early in range(heads - 1):
                to_sibling(early).wait_recv()
            lax.fori_loop(0, n_y, project_first, 0)

        return carry

    lax.fori_loop(0, heads, one_head, 0)

    reach = n_y // 2
    first_set = range(upward)
    second_set = range(upward, chains)

    def hop(way, step, chain):
        slot = (way * reach + step) * chains + chain
        return pltpu.make_async_remote_copy(
            src_ref=ring_send.at[slot],
            dst_ref=ring_recv.at[slot],
            send_sem=ring_send_sem.at[slot],
            recv_sem=ring_recv_sem.at[slot],
            device_id=(me, above if way else below),
            device_id_type=MESH,
        )

    def rows_of(o, chain):
        return sums[o, chain * GROUP_ROWS : (chain + 1) * GROUP_ROWS, :]

    def arrived(way, step, chain):
        hop(way, step, chain).wait_recv()
        return ring_recv[(way * reach + step) * chains + chain].astype(F32)

    def first_hop(way, chain, o):
        ring_send[way * reach * chains + chain] = rows_of(o, chain).astype(BF16)
        hop(way, 0, chain).start()

    def next_hop(way, step, chain, o):
        slot = (way * reach + step) * chains + chain
        ring_send[slot] = (rows_of(o, chain) + arrived(way, step - 1, chain)).astype(BF16)
        hop(way, step, chain).start()

    to_sibling(heads - 1).wait_recv()
    project_last(0, 0)
    for down, up in zip(first_set, second_set):
        first_hop(0, down, 0)
        first_hop(1, up, 0)
    lax.fori_loop(1, 3, project_last, 0)
    for down, up in zip(second_set, first_set):
        first_hop(0, down, 1)
        first_hop(1, up, 2)

    def ring_step(step, carry):
        for down, up in zip(first_set, second_set):
            next_hop(0, step, down, 2 * step - 1)
            next_hop(1, step, up, 2 * step)
        lax.fori_loop(2 * step + 1, jnp.minimum(2 * step + 3, n_y), project_last, 0)

        @pl.when(step < reach - 1)
        def _():
            for down, up in zip(second_set, first_set):
                next_hop(0, step, down, 2 * step + 1)
                next_hop(1, step, up, 2 * step + 2)

        return carry

    lax.fori_loop(1, reach, ring_step, 0)

    def back(index, target, home):
        return pltpu.make_async_remote_copy(
            src_ref=back_send.at[index],
            dst_ref=back_recv.at[home],
            send_sem=back_send_sem.at[index],
            recv_sem=back_recv_sem.at[home],
            device_id=(target, lane),
            device_id_type=MESH,
        )

    shape = (TOGETHER * PAD, GROUP_ROWS)
    to, source = iota(shape, 0), iota(shape, 1)
    apart = jnp.where(
        (source == (to >> 4) * CAP + (to & 15)) & ((to & 15) < CAP), 1.0, 0.0
    ).astype(BF16)
    for pair in range(upward):
        for chain in (pair, upward + pair):
            longer = 0 if chain in first_set else 1
            final = rows_of(n_y - 1, chain) + arrived(1 - longer, reach - 2, chain)
            final = (final + arrived(longer, reach - 1, chain)).astype(BF16)
            laid = dot(apart, final).astype(BF16)
            for i in range(TOGETHER):
                index = chain * TOGETHER + i
                target = (core * chains + chain) * TOGETHER + i
                back_send[index] = laid[i * PAD : (i + 1) * PAD]

                @pl.when(target != me)
                def _():
                    back(index, target, me).start()

                @pl.when(target == me)
                def _():
                    back_recv[me] = back_send[index]

    half_dp = n_dp // 2
    mine = (me // half_dp) == core

    def to_last():
        return pltpu.make_async_remote_copy(
            src_ref=last_send,
            dst_ref=last_recv,
            send_sem=last_sem.at[0],
            recv_sem=last_sem.at[1],
            device_id=(me, sibling),
            device_id_type=MESH,
        )

    for part in range(heads):

        def left_part(step, carry):
            other = lax.rem(me + step, n_dp)
            message(part, other, other).wait_send()
            return carry

        lax.fori_loop(1, n_dp, left_part, 0)
    for copy in far_copies:
        copy.wait_send()
    for head in range(heads):
        to_sibling(head).wait_send()

    def left_hop(step, carry):
        for chain in range(chains):
            hop(0, step, chain).wait_send()
            hop(1, step, chain).wait_send()
        return carry

    lax.fori_loop(0, reach - 1, left_hop, 0)
    for down, up in zip(first_set, second_set):
        hop(0, reach - 1, down).wait_send()
        hop(1, reach - 1, up).wait_send()

    def left_back(index, carry):
        target = core * half_dp + index

        @pl.when(target != me)
        def _():
            back(index, target, me).wait_send()

        return carry

    lax.fori_loop(0, half_dp, left_back, 0)

    @pl.when(mine)
    def _():
        width = out.shape[1]
        wide = last_send.shape[1]
        pick = jnp.where(
            iota((tokens, n_dp * PAD), 1).astype(F32) == position[:, 0:1], 1.0, 0.0
        ).astype(BF16)
        shape = (chip_cols, wide)
        from_col, to_col = iota(shape, 0), iota(shape, 1)
        other = jnp.where(
            (from_col == to_col + (1 - core) * width) & (to_col < width), 1.0, 0.0
        ).astype(BF16)
        here = jnp.where(
            (from_col == to_col + core * width) & (to_col < width), 1.0, 0.0
        ).astype(BF16)

        def wait_back(step, carry):
            home = lax.rem(me + step, n_dp)
            back(0, home, home).wait_recv()
            return carry

        lax.fori_loop(1, n_dp, wait_back, 0)
        every = back_recv[...].reshape(n_dp * PAD, chip_cols)
        rows = dot(pick, every).astype(BF16)
        last_send[...] = dot(rows, other).astype(BF16)
        to_last().start()
        out[...] = dot(rows, here)[:, :width].astype(BF16)
        to_last().wait_send()

    @pl.when(jnp.logical_not(mine))
    def _():
        to_last().wait_recv()
        out[...] = last_recv[:, : out.shape[1]]


def shards(query_rows, key_rows, value_rows, out_grad, w_query, w_key, w_value, row_image):
    n_dp = lax.axis_size("dp")
    n_tensor = lax.axis_size("tensor")
    n_y = n_tensor // 2
    tokens, cols = query_rows.shape
    features = w_query.shape[0]
    width = features // n_tensor
    chip_cols = 2 * width
    wide = (width + HEAD - 1) // HEAD * HEAD
    heads = cols // HEAD
    n_groups = n_dp // TOGETHER
    slots = n_groups * GROUP_ROWS
    chains = n_groups // 2
    hops = n_y * chains
    vmem = pl.BlockSpec(memory_space=pltpu.VMEM)
    hbm = pl.BlockSpec(memory_space=pl.ANY)
    dma = pltpu.SemaphoreType.DMA
    return pl.pallas_call(
        functools.partial(kernel, (n_dp, n_y)),
        out_shape=jax.ShapeDtypeStruct((tokens, width), BF16),
        in_specs=[vmem] * 5 + [hbm] * 3,
        out_specs=vmem,
        scratch_shapes=[
            pltpu.VMEM((n_dp, HEAD), F32),
            pltpu.VMEM((tokens, HEAD), F32),
            pltpu.VMEM((n_dp, BLOCK_ROWS, HEAD), BF16),
            pltpu.VMEM((n_dp, BLOCK_ROWS, HEAD), BF16),
            pltpu.VMEM((4, slots, HEAD), BF16),
            pltpu.VMEM((1, slots), F32),
            pltpu.VMEM((slots, HEAD), F32),
            pltpu.VMEM((heads, slots // 2, 3 * HEAD), BF16),
            pltpu.VMEM((heads, slots // 2, 3 * HEAD), BF16),
            pltpu.VMEM((heads, slots // 2, 3 * HEAD), BF16),
            pltpu.VMEM((2, features, 3 * cols), BF16),
            pltpu.VMEM((n_y, slots // 2, chip_cols), F32),
            pltpu.VMEM((hops, GROUP_ROWS, chip_cols), BF16),
            pltpu.VMEM((hops, GROUP_ROWS, chip_cols), BF16),
            pltpu.VMEM((n_dp // 2, PAD, chip_cols), BF16),
            pltpu.VMEM((n_dp, PAD, chip_cols), BF16),
            pltpu.VMEM((tokens, wide), BF16),
            pltpu.VMEM((tokens, wide), BF16),
            dma((heads, n_dp)),
            dma((heads, n_dp)),
            dma((3,)),
            dma((3,)),
            dma((3,)),
            dma((heads,)),
            dma((heads,)),
            dma((hops,)),
            dma((hops,)),
            dma((n_dp // 2,)),
            dma((n_dp,)),
            dma((2,)),
        ],
        compiler_params=pltpu.CompilerParams(
            collective_id=0, has_side_effects=True, vmem_limit_bytes=56 * 2**20
        ),
    )(
        row_image.reshape(1, tokens),
        query_rows,
        key_rows,
        value_rows,
        out_grad,
        w_query,
        w_key,
        w_value,
    )


def solution(mesh):
    placed = (
        P("dp", "tensor"),
        P("dp", "tensor"),
        P("dp", "tensor"),
        P("dp", "tensor"),
        P(None, "tensor"),
        P(None, "tensor"),
        P(None, "tensor"),
        P("dp"),
    )
    return jax.shard_map(
        shards, mesh=mesh, in_specs=placed, out_specs=P("dp", "tensor"), check_vma=False
    )
```

time: 144 us -> 132 us (0.917)
  the two profiles are of different devices: /device:TPU:3 before, /device:TPU:91 now
where the time goes in v2:
time: 132 us
  Pallas kernels  130 us (98%)
  local copies, waits for them, and re-layouts  1.65 us (1%)
    pallas_call x1, Pallas kernels, shards(): pl.pallas_call(functools.partial(kernel, (n_dp, n_y)), out_shape=jax.Shap...  130 us

profile of v2, /device:TPU:91, one launch (start us, length us, event | category | flops | bytes accessed | tf_op | source)
XLA Modules:
  0.0 131.6 jit_solution(7280152730653285122)
XLA Ops:
  0.0 129.9 %shard_map.82 = bf16[256,192]{1,0:T(8,128)(2,1)} custom-call(s32[1,256]{1,0:T(1,128)} %bitcast.1, bf16[256,384]{1,0:T(8,128)(2,1)} %query.1, bf16[256,384]{1,0:T(8,128)(2,1)} %key.1, bf16[256,384]{1,0:T(8,128)(2,1)} %value.1, bf16[256,384]{1,0:T(8,128)(2,1)} %grad.1, bf16[3072,384]{1,0:T(8,128)(2,1)} %w_query.1, bf16[3072,384]{1,0:T(8,128)(2,1)} %w_key.1, ...), custom_call_target="tpu_custom_call" | custom-call | tf_op jit(solution)/shard_map/pallas_call | solution.py:550
  129.9 1.6 %copy.9 = bf16[256,192]{0,1:T(8,128)(2,1)} copy(bf16[256,192]{1,0:T(8,128)(2,1)} %shard_map.82) | data formatting | bytes 196608 | tf_op jit(solution)/shard_map/pallas_call | solution.py:550

commit v3 on v2

--- a/solution.py
+++ b/solution.py
@@ -14,7 +14,7 @@
 TOGETHER = 6
 WINDOW = 32
 BLOCK_ROWS = 160
-PARTS = ((0, 64), (64, 48), (112, 48))
+PARTS = ((0, 112), (112, 48))
 GROUP_ROWS = 80
 MESH = pl.DeviceIdType.MESH
 F32 = jnp.float32
@@ -40,6 +40,7 @@
     w_key,
     w_value,
     out,
+    rows_in,
     codes,
     position,
     send,
@@ -58,6 +59,7 @@
     back_recv,
     last_send,
     last_recv,
+    row_sem,
     send_sem,
     recv_sem,
     weight_sem,
@@ -105,6 +107,13 @@
     for other in (sibling, above, below):
         pl.semaphore_signal(barrier, inc=1, device_id=(me, other), device_id_type=MESH)
 
+    row_copies = [
+        pltpu.make_async_copy(source, rows_in.at[i], row_sem.at[i])
+        for i, source in enumerate((query, key, value, grad))
+    ]
+    for copy in row_copies:
+        copy.start()
+
     sources = (w_query, w_key, w_value)
     weight_copies = [
         pltpu.make_async_copy(
@@ -160,15 +169,22 @@
             device_id_type=MESH,
         )
 
+    def target_of(k):
+        away = k // 2 + 1
+        away = jnp.where(k % 2 == 0, away, n_dp - away)
+        return lax.rem(me + jnp.where(k == n_dp - 1, 0, away), n_dp)
+
+    for copy in row_copies:
+        copy.wait()
     pl.semaphore_wait(barrier, n_dp + 2)
 
     def pack(step, carry):
-        targets = [lax.rem(me + 1 + step * TOGETHER + i, n_dp) for i in range(TOGETHER)]
+        targets = [target_of(step * TOGETHER + i) for i in range(TOGETHER)]
         wanted = jnp.concatenate(
             [iota((PAD, tokens), 0) + target * PAD for target in targets], axis=0
         ).astype(F32)
         pick = jnp.where(wanted == placed_r, 1.0, 0.0).astype(BF16)
-        parts = [dot(pick, ref[...]).astype(BF16) for ref in (query, key, value, grad)]
+        parts = [dot(pick, ref[...]).astype(BF16) for ref in (rows_in.at[n] for n in range(4))]
         rows = []
         for head in range(heads):
             for part in parts:
@@ -196,13 +212,13 @@
     lax.fori_loop(0, n_groups, pack, 0)
     for copy in weight_copies + far_copies:
         copy.start()
-    for part in range(1, heads):
+    for part in range(1, len(PARTS)):
 
         def start_part(step, carry):
-            message(part, me, lax.rem(me + step, n_dp)).start()
+            message(part, me, target_of(step)).start()
             return carry
 
-        lax.fori_loop(1, n_dp, start_part, 0)
+        lax.fori_loop(0, n_dp - 1, start_part, 0)
     recv[me] = send[me]
     position[...] = jnp.transpose(jnp.broadcast_to(placed_r, (HEAD, tokens)))
 
@@ -327,9 +343,9 @@
         return carry
 
     def one_head(head, carry):
-        for part in range(heads):
-
-            @pl.when(head == part)
+        for part in range(len(PARTS)):
+
+            @pl.when(head == part * (heads - 1))
             def _():
                 def wait_part(step, carry):
                     other = lax.rem(me + step, n_dp)
@@ -460,7 +476,7 @@
             device_id_type=MESH,
         )
 
-    for part in range(heads):
+    for part in range(len(PARTS)):
 
         def left_part(step, carry):
             other = lax.rem(me + step, n_dp)
@@ -502,15 +518,6 @@
         pick = jnp.where(
             iota((tokens, n_dp * PAD), 1).astype(F32) == position[:, 0:1], 1.0, 0.0
         ).astype(BF16)
-        shape = (chip_cols, wide)
-        from_col, to_col = iota(shape, 0), iota(shape, 1)
-        other = jnp.where(
-            (from_col == to_col + (1 - core) * width) & (to_col < width), 1.0, 0.0
-        ).astype(BF16)
-        here = jnp.where(
-            (from_col == to_col + core * width) & (to_col < width), 1.0, 0.0
-        ).astype(BF16)
-
         def wait_back(step, carry):
             home = lax.rem(me + step, n_dp)
             back(0, home, home).wait_recv()
@@ -518,16 +525,35 @@
 
         lax.fori_loop(1, n_dp, wait_back, 0)
         every = back_recv[...].reshape(n_dp * PAD, chip_cols)
-        rows = dot(pick, every).astype(BF16)
-        last_send[...] = dot(rows, other).astype(BF16)
-        to_last().start()
-        out[...] = dot(rows, here)[:, :width].astype(BF16)
+        rows = dot(pick, every)
+
+        @pl.when(core == 0)
+        def _():
+            last_send[...] = rows[:, chip_cols - wide :].astype(BF16)
+            to_last().start()
+            out[...] = rows[:, :width].astype(BF16)
+
+        @pl.when(core == 1)
+        def _():
+            last_send[...] = rows[:, :wide].astype(BF16)
+            to_last().start()
+            out[...] = rows[:, width:].astype(BF16)
+
         to_last().wait_send()
 
     @pl.when(jnp.logical_not(mine))
     def _():
+        width = out.shape[1]
+        wide = last_recv.shape[1]
         to_last().wait_recv()
-        out[...] = last_recv[:, : out.shape[1]]
+
+        @pl.when(core == 0)
+        def _():
+            out[...] = last_recv[:, :width]
+
+        @pl.when(core == 1)
+        def _():
+            out[...] = last_recv[:, wide - width :]
 
 
 def shards(query_rows, key_rows, value_rows, out_grad, w_query, w_key, w_value, row_image):
@@ -550,9 +576,10 @@
     return pl.pallas_call(
         functools.partial(kernel, (n_dp, n_y)),
         out_shape=jax.ShapeDtypeStruct((tokens, width), BF16),
-        in_specs=[vmem] * 5 + [hbm] * 3,
+        in_specs=[vmem] + [hbm] * 7,
         out_specs=vmem,
         scratch_shapes=[
+            pltpu.VMEM((4, tokens, cols), BF16),
             pltpu.VMEM((n_dp, HEAD), F32),
             pltpu.VMEM((tokens, HEAD), F32),
             pltpu.VMEM((n_dp, BLOCK_ROWS, HEAD), BF16),
@@ -571,8 +598,9 @@
             pltpu.VMEM((n_dp, PAD, chip_cols), BF16),
             pltpu.VMEM((tokens, wide), BF16),
             pltpu.VMEM((tokens, wide), BF16),
-            dma((heads, n_dp)),
-            dma((heads, n_dp)),
+            dma((4,)),
+            dma((len(PARTS), n_dp)),
+            dma((len(PARTS), n_dp)),
             dma((3,)),
             dma((3,)),
             dma((3,)),

time: 132 us -> 129 us (0.977)
  the two profiles are of different devices: /device:TPU:91 before, /device:TPU:95 now
where the time goes in v3:
time: 129 us; the launch traced here: 128 us
  Pallas kernels  127 us (98%)
  local copies, waits for them, and re-layouts  1.65 us (1%)
    pallas_call x1, Pallas kernels, shards(): pl.pallas_call(functools.partial(kernel, (n_dp, n_y)), out_shape=jax.Shap...  127 us

profile of v3, /device:TPU:95, one launch (start us, length us, event | category | flops | bytes accessed | tf_op | source)
XLA Modules:
  0.0 128.5 jit_solution(8833345673056095913)
XLA Ops:
  0.0 126.8 %shard_map.82 = bf16[256,192]{1,0:T(8,128)(2,1)} custom-call(s32[1,256]{1,0:T(1,128)} %bitcast.1, bf16[256,384]{1,0:T(8,128)(2,1)} %query.1, bf16[256,384]{1,0:T(8,128)(2,1)} %key.1, bf16[256,384]{1,0:T(8,128)(2,1)} %value.1, bf16[256,384]{1,0:T(8,128)(2,1)} %grad.1, bf16[3072,384]{1,0:T(8,128)(2,1)} %w_query.1, bf16[3072,384]{1,0:T(8,128)(2,1)} %w_key.1, ...), custom_call_target="tpu_custom_call" | custom-call | tf_op jit(solution)/shard_map/pallas_call | solution.py:576
  126.8 1.6 %copy.9 = bf16[256,192]{0,1:T(8,128)(2,1)} copy(bf16[256,192]{1,0:T(8,128)(2,1)} %shard_map.82) | data formatting | bytes 196608 | tf_op jit(solution)/shard_map/pallas_call | solution.py:576

commit v4 on v3

--- a/solution.py
+++ b/solution.py
@@ -342,6 +342,14 @@
         sums[o] += product(grad_mine, 0, o, some) + product(grad_recv, 1, o, some)
         return carry
 
+    def left_part(part):
+        def left_one(step, carry):
+            other = lax.rem(me + step, n_dp)
+            message(part, other, other).wait_send()
+            return carry
+
+        lax.fori_loop(1, n_dp, left_one, 0)
+
     def one_head(head, carry):
         for part in range(len(PARTS)):
 
@@ -367,6 +375,10 @@
             for early in range(heads - 1):
                 to_sibling(early).wait_recv()
             lax.fori_loop(0, n_y, project_first, 0)
+            for part in range(len(PARTS) - 1):
+                left_part(part)
+            for copy in far_copies:
+                copy.wait_send()
 
         return carry
 
@@ -476,40 +488,32 @@
             device_id_type=MESH,
         )
 
-    for part in range(len(PARTS)):
-
-        def left_part(step, carry):
-            other = lax.rem(me + step, n_dp)
-            message(part, other, other).wait_send()
+    def drain():
+        left_part(len(PARTS) - 1)
+        for head in range(heads):
+            to_sibling(head).wait_send()
+
+        def left_hop(step, carry):
+            for chain in range(chains):
+                hop(0, step, chain).wait_send()
+                hop(1, step, chain).wait_send()
             return carry
 
-        lax.fori_loop(1, n_dp, left_part, 0)
-    for copy in far_copies:
-        copy.wait_send()
-    for head in range(heads):
-        to_sibling(head).wait_send()
-
-    def left_hop(step, carry):
-        for chain in range(chains):
-            hop(0, step, chain).wait_send()
-            hop(1, step, chain).wait_send()
-        return carry
-
-    lax.fori_loop(0, reach - 1, left_hop, 0)
-    for down, up in zip(first_set, second_set):
-        hop(0, reach - 1, down).wait_send()
-        hop(1, reach - 1, up).wait_send()
-
-    def left_back(index, carry):
-        target = core * half_dp + index
-
-        @pl.when(target != me)
-        def _():
-            back(index, target, me).wait_send()
-
-        return carry
-
-    lax.fori_loop(0, half_dp, left_back, 0)
+        lax.fori_loop(0, reach - 1, left_hop, 0)
+        for down, up in zip(first_set, second_set):
+            hop(0, reach - 1, down).wait_send()
+            hop(1, reach - 1, up).wait_send()
+
+        def left_back(index, carry):
+            target = core * half_dp + index
+
+            @pl.when(target != me)
+            def _():
+                back(index, target, me).wait_send()
+
+            return carry
+
+        lax.fori_loop(0, half_dp, left_back, 0)
 
     @pl.when(mine)
     def _():
@@ -539,12 +543,14 @@
             to_last().start()
             out[...] = rows[:, width:].astype(BF16)
 
+        drain()
         to_last().wait_send()
 
     @pl.when(jnp.logical_not(mine))
     def _():
         width = out.shape[1]
         wide = last_recv.shape[1]
+        drain()
         to_last().wait_recv()
 
         @pl.when(core == 0)

time: 129 us -> 129 us (level)
  no operation moved by 1% of the time
where the time goes in v4:
time: 129 us; the launch traced here: 128 us
  Pallas kernels  127 us (98%)
  local copies, waits for them, and re-layouts  1.65 us (1%)
    pallas_call x1, Pallas kernels, shards(): pl.pallas_call(functools.partial(kernel, (n_dp, n_y)), out_shape=jax.Shap...  127 us

profile of v4, /device:TPU:95, one launch (start us, length us, event | category | flops | bytes accessed | tf_op | source)
XLA Modules:
  0.0 128.5 jit_solution(3015742008317525055)
XLA Ops:
  0.0 126.8 %shard_map.82 = bf16[256,192]{1,0:T(8,128)(2,1)} custom-call(s32[1,256]{1,0:T(1,128)} %bitcast.1, bf16[256,384]{1,0:T(8,128)(2,1)} %query.1, bf16[256,384]{1,0:T(8,128)(2,1)} %key.1, bf16[256,384]{1,0:T(8,128)(2,1)} %value.1, bf16[256,384]{1,0:T(8,128)(2,1)} %grad.1, bf16[3072,384]{1,0:T(8,128)(2,1)} %w_query.1, bf16[3072,384]{1,0:T(8,128)(2,1)} %w_key.1, ...), custom_call_target="tpu_custom_call" | custom-call | tf_op jit(solution)/shard_map/pallas_call | solution.py:582
  126.8 1.6 %copy.9 = bf16[256,192]{0,1:T(8,128)(2,1)} copy(bf16[256,192]{1,0:T(8,128)(2,1)} %shard_map.82) | data formatting | bytes 196608 | tf_op jit(solution)/shard_map/pallas_call | solution.py:582
